TPU v7x, 128 devices: a whole 4x4x4 slice. The times are simulated.
128 devices in a mesh: doc: 8 (over y, x_hi), cent: 16 (over z, x_lo, core).
Axes of the slice: x: 4 (x_hi: 2, x_lo: 2; x = x_hi * 2 + x_lo), y: 4, z: 4, core: 2. Of those that a mesh axis runs over, the one named last changes fastest.
Arguments:
- embeddings: float32 [65536, 1024], P(('doc', 'cent'))
- centroids: float32 [16384, 1024], P('cent')
- cluster: int32 [65536], P(('doc', 'cent')), may hold values from 0 to 16383, as said below
- slot: int32 [65536], P(('doc', 'cent')), may hold values from 0 to 7, as said below
Outputs:
- soft_cost: float32 [65536], P(('doc', 'cent'))
- dup_sim: float32 [65536], P(('doc', 'cent'))
Inputs may be any that keep to these rules, and one draw needn't show every extreme that they name: Owner device of row r is cluster[r] // 128; some owner device receives rows from every device. `slot`: slots of the rows of one device that have the same owner device are distinct; in every draw some owner device takes 8 rows from every device.
All inputs are finite; a program needn't handle non-finite values.
Results may differ from a plain program's by a relative error of at most 0.0003.
Values may be sent and summed in bfloat16 or wider, within the bound.
No kernel may reach another device: no remote copies, remote signals or barrier semaphores. Data moves between devices by JAX's collectives and lax.ppermute only.
A program may use at most 192 MiB of HBM per device.

v0:
```python
import jax
import jax.numpy as jnp
from jax import lax
from jax.sharding import PartitionSpec as P

inverse_temp = 256.0


def unit_rows(values):
    total = jnp.sum(values * values, axis=1, keepdims=True)
    return (values * lax.rsqrt(total + 1e-06)).astype(jnp.bfloat16)


def inner_rows(left, right):
    return lax.dot_general(
        left, right, (((1,), (1,)), ((), ())), preferred_element_type=jnp.float32
    )


def block_terms(part, centre):
    score = inner_rows(part, centre) * inverse_temp
    high = jnp.max(score, axis=1)
    return (high, jnp.sum(jnp.exp(score - high[:, None]), axis=1))


def join_terms(first, second):
    high = jnp.maximum(first[0], second[0])
    return (high, second[1] * jnp.exp(second[0] - high))


def owner_best(rows, ids):
    total = rows.shape[0]
    block = min(512, total)
    col_pos = jnp.arange(total)

    def one_block(index):
        start = index * block
        part = lax.dynamic_slice_in_dim(rows, start, block, 0)
        part_ids = lax.dynamic_slice_in_dim(ids, start, block, 0)
        gram = inner_rows(part, rows)
        row_pos = start + jnp.arange(block)
        mask = (
            (part_ids[:, None] == ids[None, :])
            & (ids[None, :] >= 0.0)
            & (col_pos[None, :] < row_pos[:, None])
        )
        return jnp.max(jnp.where(mask, gram, jnp.float32(-1.0)), axis=1)

    return lax.map(one_block, jnp.arange(total // block)).reshape(total)


def per_device(embeddings, centroids, cluster, slot):
    row_count, width = embeddings.shape
    doc_count = lax.axis_size("doc")
    cent_count = lax.axis_size("cent")
    devices = doc_count * cent_count
    per_owner = centroids.shape[0] // doc_count
    capacity = 2 * row_count // devices
    unit = unit_rows(embeddings)
    centre = unit_rows(centroids)
    start_terms = (jnp.full((row_count,), -1e30, jnp.float32), jnp.zeros((row_count,), jnp.float32))
    high, total = join_terms(
        start_terms, block_terms(unit, lax.all_gather(centre, "cent", axis=0, tiled=True))
    )
    soft_cost = 1.0 - (high + jnp.log(total)) / inverse_temp
    owner = cluster // per_owner
    local = (cluster % per_owner).astype(jnp.bfloat16)
    target = owner * capacity + slot
    send_rows = jnp.zeros((devices * capacity, width), jnp.bfloat16).at[target].set(unit)
    send_ids = jnp.full((devices * capacity,), -1.0, jnp.bfloat16).at[target].set(local)
    got_rows, got_ids = (
        lax.all_to_all(
            send_rows.reshape(devices, capacity, width),
            ("doc", "cent"),
            split_axis=0,
            concat_axis=0,
            tiled=True,
        ),
        lax.all_to_all(
            send_ids.reshape(devices, capacity),
            ("doc", "cent"),
            split_axis=0,
            concat_axis=0,
            tiled=True,
        ),
    )
    best = owner_best(
        got_rows.reshape(devices * capacity, width),
        got_ids.reshape(devices * capacity).astype(jnp.float32),
    )
    returned = lax.all_to_all(
        best.reshape(devices, capacity), ("doc", "cent"), split_axis=0, concat_axis=0, tiled=True
    )
    dup_sim = returned.reshape(devices * capacity)[target]
    return (soft_cost, dup_sim)


def solution(mesh):
    return jax.shard_map(
        per_device,
        mesh=mesh,
        in_specs=(
            P(("doc", "cent"), None),
            P("cent", None),
            P(("doc", "cent")),
            P(("doc", "cent")),
        ),
        out_specs=(P(("doc", "cent")), P(("doc", "cent"))),
        check_vma=False,
    )
```

profile of v0, /device:TPU:1, one launch (start us, length us, event | category | flops | bytes accessed | tf_op | source)
XLA Modules:
  0.0 260.8 jit_solution(17680688221776090694)
XLA Ops:
  7.2 2.7 %multiply_reduce_fusion.1 = f32[1024]{0:T(1024)S(1)} fusion(f32[1024,1024]{1,0:T(8,128)} %param.7), kind=kLoop, calls=%fused_computation.14 | loop fusion | flops 2096128 | bytes 4198400 | tf_op jit(solution)/shard_map/reduce_sum | solution.py:10
  9.9 0.7 copy-done
  10.7 1.6 multiply_convert_fusion
  12.3 0.6 copy-done.2
  13.0 3.8 %scatter_custom_fusion = bf16[1024]{0:T(1024)(128)(2,1)S(1)} fusion(s32[512]{0:T(512)S(1)} %get-tuple-element.58, bf16[512]{0:T(512)(128)(2,1)S(1)} %get-tuple-element.57, bf16[]{:T(256)} %constant.72.clone.1), kind=kCustom, calls=%fused_computation.42 | custom fusion | bytes 2050 | tf_op jit(solution)/shard_map/scatter | solution.py:70
  16.7 0.8 all_to_all.20
  17.5 11.5 %all-to-all-start = ((bf16[128,1,8]{2,1,0:T(2,128)(2,1)}), bf16[128,1,8]{2,1,0:T(2,128)(2,1)S(1)}, u32[]{:S(2)}, u32[]{:S(2)}) async-start(bf16[128,1,8]{2,1,0:T(2,128)(2,1)} %all_to_all.20), calls=%async_computation | async-start | bytes 131072 | tf_op jit(solution)/shard_map/all_to_all | solution.py:79
  29.2 4.2 %scatter_custom_fusion.1 = bf16[1024,1024]{1,0:T(8,128)(2,1)} fusion(s32[512]{0:T(512)S(1)} %get-tuple-element.58, bf16[]{:T(256)} %constant.65.clone.1, f32[512,1024]{1,0:T(8,128)S(1)} %copy-done.1, f32[512]{0:T(512)S(1)} %add_rsqrt_fusion.1), kind=kCustom, calls=%fused_computation.17 | custom fusion | flops 1048576 | bytes 4196354 | tf_op jit(solution)/shard_map/scatter | solution.py:69
  33.5 5.4 %all-to-all-done = bf16[128,1,8]{2,1,0:T(2,128)(2,1)S(1)} async-done(((bf16[128,1,8]{2,1,0:T(2,128)(2,1)}), bf16[128,1,8]{2,1,0:T(2,128)(2,1)S(1)}, u32[]{:S(2)}, u32[]{:S(2)}) %all-to-all-start) | async-done | bytes 2080 | tf_op jit(solution)/shard_map/all_to_all | solution.py:79
  38.8 5.3 %all-to-all-start.1 = ((bf16[128,8,1024]{2,1,0:T(8,128)(2,1)}), bf16[128,8,1024]{2,1,0:T(8,128)(2,1)}, u32[]{:S(2)}, u32[]{:S(2)}) async-start(bf16[128,8,1024]{2,1,0:T(8,128)(2,1)} %bitcast.13), calls=%async_computation.1 | async-start | bytes 4194304 | tf_op jit(solution)/shard_map/all_to_all | solution.py:72
  44.5 52.5 %all-to-all-done.1 = bf16[128,8,1024]{2,1,0:T(8,128)(2,1)} async-done(((bf16[128,8,1024]{2,1,0:T(8,128)(2,1)}), bf16[128,8,1024]{2,1,0:T(8,128)(2,1)}, u32[]{:S(2)}, u32[]{:S(2)}) %all-to-all-start.1) | async-done | bytes 2097184 | tf_op jit(solution)/shard_map/all_to_all | solution.py:72
  97.0 10.0 %while.11 = (s32[]{:T(128)}, f32[2,512]{1,0:T(2,128)S(1)}, s32[2]{0:T(128)S(1)}, f32[1024]{0:T(1024)S(1)}, bf16[1024,1024]{1,0:T(8,128)(2,1)}, /*index=5*/s32[]{:T(128)}, s32[1]{0:T(128)}, s32[]{:T(128)}, s32[]{:T(128)}) while((s32[]{:T(128)}, f32[2,512]{1,0:T(2,128)S(1)}, s32[2]{0:T(128)S(1)}, f32[1024]{0:T(1024)S(1)}, ...), condition=%wide.region_8.9_spmd.clone, body=%wide.region_6.8_spmd.clone.sunk | while | flops 1076888576 | bytes 3172527 | solution.py:49
  98.3 3.6 %select_reduce_fusion.2 = f32[512]{0:T(512)S(1)} fusion(bf16[1024,1024]{1,0:T(8,128)(2,1)} %get-tuple-element.114, s32[]{:T(128)S(6)} %select_n.45, s32[512]{0:T(512)S(1)} %iota_add_fusion.2, f32[1024]{0:T(1024)S(1)} %get-tuple-element.113, f32[512]{0:T(512)S(1)} %dynamic_slice.20, pred[1024]{0:T(1024)(128)(4,1)S(1)} %broadcast_compare_fusion.3), kind=kOutput, calls=%fused_computation.5.clone.1 | convolution fusion | flops 1076887040 | bytes 3156996 | tf_op jit(solution)/shard_map/while/body/eval_jaxpr/dot_general | solution.py:15
  102.0 0.6 dynamic_slice.19
  103.3 3.6 %select_reduce_fusion.2 = f32[512]{0:T(512)S(1)} fusion(bf16[1024,1024]{1,0:T(8,128)(2,1)} %get-tuple-element.114, s32[]{:T(128)S(6)} %select_n.45, s32[512]{0:T(512)S(1)} %iota_add_fusion.2, f32[1024]{0:T(1024)S(1)} %get-tuple-element.113, f32[512]{0:T(512)S(1)} %dynamic_slice.20, pred[1024]{0:T(1024)(128)(4,1)S(1)} %broadcast_compare_fusion.3), kind=kOutput, calls=%fused_computation.5.clone.1 | convolution fusion | flops 1076887040 | bytes 3156996 | tf_op jit(solution)/shard_map/while/body/eval_jaxpr/dot_general | solution.py:15
  106.9 0.7 all_to_all.18
  107.7 4.5 %all-to-all-start.2 = ((f32[128,1,8]{2,1,0:T(1,128)}), f32[128,1,8]{2,1,0:T(1,128)S(1)}, u32[]{:S(2)}, u32[]{:S(2)}) async-start(f32[128,1,8]{2,1,0:T(1,128)} %bitcast.2), calls=%async_computation.2 | async-start | bytes 131072 | tf_op jit(solution)/shard_map/all_to_all | solution.py:91
  112.2 9.9 %all-to-all-done.2 = f32[128,1,8]{2,1,0:T(1,128)S(1)} async-done(((f32[128,1,8]{2,1,0:T(1,128)}), f32[128,1,8]{2,1,0:T(1,128)S(1)}, u32[]{:S(2)}, u32[]{:S(2)}) %all-to-all-start.2) | async-done | bytes 4128 | tf_op jit(solution)/shard_map/all_to_all | solution.py:91
  122.7 0.8 reduce.7
  123.6 3.4 %gather_fusion = f32[512]{0:T(512)} fusion(f32[1024]{0:T(1024)S(1)} %reshape.53, s32[1024]{0:T(1024)S(1)} %pad_clamp_fusion), kind=kCustom, calls=%fused_computation | custom fusion | bytes 6144 | tf_op jit(solution)/shard_map/gather | solution.py:94
  127.0 83.6 %all-gather.2.cloned.1.call-done = bf16[16384,1024]{1,0:T(8,128)(2,1)} async-done(((bf16[1024,1024]{1,0:T(8,128)(2,1)}), bf16[16384,1024]{1,0:T(8,128)(2,1)}) %all-gather.2.cloned.1.call-update) | async-done | bytes 33554448 | tf_op jit(solution)/shard_map/all_gather | solution.py:63
  210.6 28.6 %multiply_reduce_fusion = (f32[512]{0:T(512)S(1)}, f32[512,16384]{1,0:T(8,128)}) fusion(bf16[16384,1024]{1,0:T(8,128)(2,1)} %all-gather.2.cloned.1.call-done, f32[512,1024]{1,0:T(8,128)S(1)} %copy-done.1, f32[512]{0:T(512)S(1)} %add_rsqrt_fusion.1), kind=kOutput, calls=%fused_computation.12 | convolution fusion | flops 17197694976 | bytes 69210112 | tf_op jit(solution)/shard_map/dot_general | solution.py:15
  239.2 14.1 %exponential_reduce_fusion = f32[512]{0:T(512)S(1)} fusion(f32[512,16384]{1,0:T(8,128)} %get-tuple-element.60, f32[512]{0:T(512)S(1)} %get-tuple-element.59), kind=kLoop, calls=%fused_computation.11 | loop fusion | flops 25165312 | bytes 33558528 | tf_op jit(solution)/shard_map/reduce_sum | solution.py:23
  253.3 0.6 fusion.11
  (28 shorter events, 2.0 us)
Async XLA Ops:
  7.2 203.4 %all-gather.2.cloned.1.call-start = ((), (), s32[]{:S(2)}) async-start(), calls=%async_computation.3 | async-start | bytes 35651584 | tf_op jit(solution)/shard_map/all_gather | solution.py:63
  7.2 3.5 %copy-start = (f32[1024,1024]{1,0:T(8,128)S(1)}, f32[1024,1024]{1,0:T(8,128)}, u32[]{:S(2)}) copy-start(f32[1024,1024]{1,0:T(8,128)} %param.7) | copy-start | bytes 12582916
  10.7 1.6 copy-start.3
  12.3 0.7 copy-start.2
  12.3 16.7 %copy-start.1 = (f32[512,1024]{1,0:T(8,128)S(1)}, f32[512,1024]{1,0:T(8,128)}, u32[]{:S(2)}) copy-start(f32[512,1024]{1,0:T(8,128)} %param.6) | copy-start | bytes 6291460
  17.5 21.3 %all-to-all-start = ((bf16[128,1,8]{2,1,0:T(2,128)(2,1)}), bf16[128,1,8]{2,1,0:T(2,128)(2,1)S(1)}, u32[]{:S(2)}, u32[]{:S(2)}) async-start(bf16[128,1,8]{2,1,0:T(2,128)(2,1)} %all_to_all.20), calls=%async_computation | async-start | bytes 131072 | tf_op jit(solution)/shard_map/all_to_all | solution.py:79
  38.8 58.1 %all-to-all-start.1 = ((bf16[128,8,1024]{2,1,0:T(8,128)(2,1)}), bf16[128,8,1024]{2,1,0:T(8,128)(2,1)}, u32[]{:S(2)}, u32[]{:S(2)}) async-start(bf16[128,8,1024]{2,1,0:T(8,128)(2,1)} %bitcast.13), calls=%async_computation.1 | async-start | bytes 4194304 | tf_op jit(solution)/shard_map/all_to_all | solution.py:72
  107.7 14.5 %all-to-all-start.2 = ((f32[128,1,8]{2,1,0:T(1,128)}), f32[128,1,8]{2,1,0:T(1,128)S(1)}, u32[]{:S(2)}, u32[]{:S(2)}) async-start(f32[128,1,8]{2,1,0:T(1,128)} %bitcast.2), calls=%async_computation.2 | async-start | bytes 131072 | tf_op jit(solution)/shard_map/all_to_all | solution.py:91
Sparse Core Ops, SparseCore 0:
  12.4 198.1 all-gather.1
where the time goes:
time: 261 us
  waiting for transfers between devices  151 us (58%)
  matrix products  35.8 us (14%)
  other arithmetic  24.4 us (9%)
  starting transfers between devices  21.4 us (8%)
  between operations  14.1 us (5%)
  local copies, waits for them, and re-layouts  12.2 us (5%)
    all_gather x1, waiting for transfers between devices, per_device(): lax.all_gather(centre, 'cent', axis=0, tiled=True)  83.6 us
    all_to_all x1, waiting for transfers between devices, per_device(): lax.all_to_all(send_rows.reshape(devices, capacity, width), ('doc', 'cent...  52.5 us
    dot_general x3, matrix products, inner_rows(): lax.dot_general(left, right, (((1,), (1,)), ((), ())), preferred_element_...  35.8 us
    reduce_sum x1, other arithmetic, block_terms(): return (high, jnp.sum(jnp.exp(score - high[:, None]), axis=1))  14.1 us
    all_to_all x1, starting transfers between devices, per_device(): lax.all_to_all(send_ids.reshape(devices, capacity), ('doc', 'cent'), spli...  11.5 us
    all_to_all x1, waiting for transfers between devices, per_device(): lax.all_to_all(best.reshape(devices, capacity), ('doc', 'cent'), split_ax...  9.95 us
    all_to_all x1, waiting for transfers between devices, per_device(): lax.all_to_all(send_ids.reshape(devices, capacity), ('doc', 'cent'), spli...  5.37 us
    all_to_all x1, starting transfers between devices, per_device(): lax.all_to_all(send_rows.reshape(devices, capacity, width), ('doc', 'cent...  5.32 us
  transfers between devices with their start and end apart: 4, of which 4 were waited for; matrix products, arithmetic and copies ran while one was open for 8% of the time, Pallas kernels for 0%

commit v1 on v0

--- a/solution.py
+++ b/solution.py
@@ -4,6 +4,11 @@
 from jax.sharding import PartitionSpec as P
 
 inverse_temp = 256.0
+
+
+def swapped_in(shard, mesh_axis, dim):
+    outgoing = jnp.stack([shard] * lax.axis_size(mesh_axis))
+    return jnp.concatenate(lax.all_to_all(outgoing, mesh_axis, 0, 0), axis=dim)
 
 
 def unit_rows(values):
@@ -59,9 +64,7 @@
     unit = unit_rows(embeddings)
     centre = unit_rows(centroids)
     start_terms = (jnp.full((row_count,), -1e30, jnp.float32), jnp.zeros((row_count,), jnp.float32))
-    high, total = join_terms(
-        start_terms, block_terms(unit, lax.all_gather(centre, "cent", axis=0, tiled=True))
-    )
+    high, total = join_terms(start_terms, block_terms(unit, swapped_in(centre, "cent", 0)))
     soft_cost = 1.0 - (high + jnp.log(total)) / inverse_temp
     owner = cluster // per_owner
     local = (cluster % per_owner).astype(jnp.bfloat16)

time: 261 us -> 516 us (1.98)
  waiting for transfers between devices: 151 us -> 397 us
  between operations: 14.1 us -> 0.73 us
  local copies, waits for them, and re-layouts: 12.2 us -> 22.9 us
  starting transfers between devices: 21.4 us -> 28.8 us
    all_to_all x0 -> x1, waiting for transfers between devices: none -> 360 us  [swapped_in(): return jnp.concatenate(lax.all_to_all(outgoing, mesh_axis, 0, 0), axis=dim)]
    all_gather x1 -> x0, waiting for transfers between devices: 83.6 us -> none  [per_device(): lax.all_gather(centre, 'cent', axis=0, tiled=True)]
    all_to_all x1, waiting for transfers between devices: 52.5 us -> 27.1 us  [per_device(): lax.all_to_all(send_rows.reshape(devices, capacity, width), ('doc', 'cent...]
    another operation x0 -> x1, local copies, waits for them, and re-layouts: none -> 12.2 us  [swapped_in(): outgoing = jnp.stack([shard] * lax.axis_size(mesh_axis))]
    all_to_all x0 -> x1, starting transfers between devices: none -> 6.31 us  [swapped_in(): return jnp.concatenate(lax.all_to_all(outgoing, mesh_axis, 0, 0), axis=dim)]
  transfers between devices with their start and end apart: 4 -> 4, of which waited for: 4 -> 4; matrix products, arithmetic and copies ran while one was open for 8% -> 3% of each run, Pallas kernels for 0% -> 0%
where the time goes in v1:
time: 516 us; the launch traced here: 515 us
  waiting for transfers between devices  397 us (77%)
  matrix products  35.8 us (7%)
  other arithmetic  28.9 us (6%)
  starting transfers between devices  28.8 us (6%)
  local copies, waits for them, and re-layouts  22.9 us (4%)
    all_to_all x1, waiting for transfers between devices, swapped_in(): return jnp.concatenate(lax.all_to_all(outgoing, mesh_axis, 0, 0), axis=dim)  360 us
    dot_general x3, matrix products, inner_rows(): lax.dot_general(left, right, (((1,), (1,)), ((), ())), preferred_element_...  35.8 us
    all_to_all x1, waiting for transfers between devices, per_device(): lax.all_to_all(send_rows.reshape(devices, capacity, width), ('doc', 'cent...  27.1 us
    reduce_sum x1, other arithmetic, block_terms(): return (high, jnp.sum(jnp.exp(score - high[:, None]), axis=1))  14.1 us
    another operation x1, local copies, waits for them, and re-layouts, swapped_in(): outgoing = jnp.stack([shard] * lax.axis_size(mesh_axis))  12.2 us
    all_to_all x1, starting transfers between devices, per_device(): lax.all_to_all(send_ids.reshape(devices, capacity), ('doc', 'cent'), spli...  11.5 us
  transfers between devices with their start and end apart: 4, of which 4 were waited for; matrix products, arithmetic and copies ran while one was open for 3% of the time, Pallas kernels for 0%

profile of v1, /device:TPU:1, one launch (start us, length us, event | category | flops | bytes accessed | tf_op | source)
XLA Modules:
  0.0 515.0 jit_solution(18246347704172117958)
XLA Ops:
  0.6 0.9 fusion.14
  1.5 3.8 scatter_custom_fusion
  5.3 0.7 all_to_all.24
  6.0 11.5 %all-to-all-start.1 = ((bf16[128,1,8]{2,1,0:T(2,128)(2,1)}), bf16[128,1,8]{2,1,0:T(2,128)(2,1)S(1)}, u32[]{:S(2)}, u32[]{:S(2)}) async-start(bf16[128,1,8]{2,1,0:T(2,128)(2,1)} %all_to_all.24), calls=%async_computation.1 | async-start | bytes 131072 | tf_op jit(solution)/shard_map/all_to_all | solution.py:82
  17.5 1.8 multiply_reduce_fusion.2
  19.3 4.2 scatter_custom_fusion.1
  23.6 3.8 all-to-all-done.1
  27.3 6.5 %all-to-all-start.2 = ((bf16[128,8,1024]{2,1,0:T(8,128)(2,1)}), bf16[128,8,1024]{2,1,0:T(8,128)(2,1)}, u32[]{:S(2)}, u32[]{:S(2)}) async-start(bf16[128,8,1024]{2,1,0:T(8,128)(2,1)} %bitcast.14), calls=%async_computation.2 | async-start | bytes 4194304 | tf_op jit(solution)/shard_map/all_to_all | solution.py:75
  33.8 2.5 multiply_reduce_fusion.1
  36.6 27.1 %all-to-all-done.2 = bf16[128,8,1024]{2,1,0:T(8,128)(2,1)} async-done(((bf16[128,8,1024]{2,1,0:T(8,128)(2,1)}), bf16[128,8,1024]{2,1,0:T(8,128)(2,1)}, u32[]{:S(2)}, u32[]{:S(2)}) %all-to-all-start.2) | async-done | bytes 2097184 | tf_op jit(solution)/shard_map/all_to_all | solution.py:75
  63.7 9.9 %while.11 = (s32[]{:T(128)}, f32[2,512]{1,0:T(2,128)S(1)}, s32[2]{0:T(128)S(1)}, f32[1024]{0:T(1024)S(1)}, bf16[1024,1024]{1,0:T(8,128)(2,1)}, /*index=5*/s32[]{:T(128)}, s32[1]{0:T(128)}, s32[]{:T(128)}, s32[]{:T(128)}) while((s32[]{:T(128)}, f32[2,512]{1,0:T(2,128)S(1)}, s32[2]{0:T(128)S(1)}, f32[1024]{0:T(1024)S(1)}, ...), condition=%wide.region_8.9_spmd.clone, body=%wide.region_6.8_spmd.clone.sunk | while | flops 1076888576 | bytes 3172527 | solution.py:54
  65.1 3.6 select_reduce_fusion.2
  70.0 3.6 select_reduce_fusion.2
  73.7 0.7 all_to_all.22
  74.4 4.5 all-to-all-start.3
  78.9 3.8 multiply_convert_fusion
  82.7 6.1 %all-to-all-done.3 = f32[128,1,8]{2,1,0:T(1,128)S(1)} async-done(((f32[128,1,8]{2,1,0:T(1,128)}), f32[128,1,8]{2,1,0:T(1,128)S(1)}, u32[]{:S(2)}, u32[]{:S(2)}) %all-to-all-start.3) | async-done | bytes 4128 | tf_op jit(solution)/shard_map/all_to_all | solution.py:94
  88.8 12.2 %stack.2 = bf16[16,1024,1024]{2,1,0:T(8,128)(2,1)} broadcast(bf16[1024,1024]{1,0:T(8,128)(2,1)} %multiply_convert_fusion), dimensions={1,2} | broadcast | bytes 35651584 | tf_op jit(solution)/shard_map/stack | solution.py:10
  101.0 6.3 %all-to-all-start = ((bf16[16,1024,1024]{2,1,0:T(8,128)(2,1)}), bf16[16,1024,1024]{2,1,0:T(8,128)(2,1)}, u32[]{:S(2)}, u32[]{:S(2)}) async-start(bf16[16,1024,1024]{2,1,0:T(8,128)(2,1)} %stack.2), calls=%async_computation | async-start | bytes 67108864 | tf_op jit(solution)/shard_map/all_to_all | solution.py:11
  107.8 0.8 reduce.7
  108.7 3.4 gather_fusion
  112.2 359.5 %all-to-all-done = bf16[16,1024,1024]{2,1,0:T(8,128)(2,1)} async-done(((bf16[16,1024,1024]{2,1,0:T(8,128)(2,1)}), bf16[16,1024,1024]{2,1,0:T(8,128)(2,1)}, u32[]{:S(2)}, u32[]{:S(2)}) %all-to-all-start) | async-done | bytes 33554464 | tf_op jit(solution)/shard_map/all_to_all | solution.py:11
  471.7 28.6 %multiply_reduce_fusion = (f32[512]{0:T(512)S(1)}, f32[512,16384]{1,0:T(8,128)}) fusion(bf16[16384,1024]{1,0:T(8,128)(2,1)} %bitcast, f32[512,1024]{1,0:T(8,128)S(1)} %copy-done, f32[512]{0:T(512)S(1)} %add_rsqrt_fusion.1), kind=kOutput, calls=%fused_computation.12 | convolution fusion | flops 17197694976 | bytes 69210112 | tf_op jit(solution)/shard_map/dot_general | solution.py:20
  500.3 14.1 %exponential_reduce_fusion = f32[512]{0:T(512)S(1)} fusion(f32[512,16384]{1,0:T(8,128)} %get-tuple-element.60, f32[512]{0:T(512)S(1)} %get-tuple-element.59), kind=kLoop, calls=%fused_computation.11 | loop fusion | flops 25165312 | bytes 33558528 | tf_op jit(solution)/shard_map/reduce_sum | solution.py:28
  (22 shorter events, 2.9 us)
Async XLA Ops:
  0.6 18.7 %copy-start = (f32[512,1024]{1,0:T(8,128)S(1)}, f32[512,1024]{1,0:T(8,128)}, u32[]{:S(2)}) copy-start(f32[512,1024]{1,0:T(8,128)} %param.6) | copy-start | bytes 6291460
  6.0 21.3 %all-to-all-start.1 = ((bf16[128,1,8]{2,1,0:T(2,128)(2,1)}), bf16[128,1,8]{2,1,0:T(2,128)(2,1)S(1)}, u32[]{:S(2)}, u32[]{:S(2)}) async-start(bf16[128,1,8]{2,1,0:T(2,128)(2,1)} %all_to_all.24), calls=%async_computation.1 | async-start | bytes 131072 | tf_op jit(solution)/shard_map/all_to_all | solution.py:82
  27.3 36.4 %all-to-all-start.2 = ((bf16[128,8,1024]{2,1,0:T(8,128)(2,1)}), bf16[128,8,1024]{2,1,0:T(8,128)(2,1)}, u32[]{:S(2)}, u32[]{:S(2)}) async-start(bf16[128,8,1024]{2,1,0:T(8,128)(2,1)} %bitcast.14), calls=%async_computation.2 | async-start | bytes 4194304 | tf_op jit(solution)/shard_map/all_to_all | solution.py:75
  74.4 14.5 %all-to-all-start.3 = ((f32[128,1,8]{2,1,0:T(1,128)}), f32[128,1,8]{2,1,0:T(1,128)S(1)}, u32[]{:S(2)}, u32[]{:S(2)}) async-start(f32[128,1,8]{2,1,0:T(1,128)} %bitcast.3), calls=%async_computation.3 | async-start | bytes 131072 | tf_op jit(solution)/shard_map/all_to_all | solution.py:94
  101.0 370.7 %all-to-all-start = ((bf16[16,1024,1024]{2,1,0:T(8,128)(2,1)}), bf16[16,1024,1024]{2,1,0:T(8,128)(2,1)}, u32[]{:S(2)}, u32[]{:S(2)}) async-start(bf16[16,1024,1024]{2,1,0:T(8,128)(2,1)} %stack.2), calls=%async_computation | async-start | bytes 67108864 | tf_op jit(solution)/shard_map/all_to_all | solution.py:11
